TPU v7x, 768 devices: a whole 4x8x12 slice. The times are simulated.
768 devices in a mesh: rep: 12 (over z), fsdp: 32 (over x, y), sub: 2 (over core).
Axes of the slice: x: 4, y: 8, z: 12, core: 2. Of those that a mesh axis runs over, the one named last changes fastest.
Arguments:
- grads: bfloat16 [12, 64, 3584, 288], P('rep', None, ('fsdp', 'sub')), may hold values from -6 to 6
- momentum: bfloat16 [64, 3584, 288], P(None, ('fsdp', 'sub')), may hold values from -18 to 18
- owner: int32 [64], replicated, may hold values from 0 to 63, each once
Outputs:
- new_momentum: bfloat16 [64, 3584, 288], P(None, ('fsdp', 'sub'))
- update: bfloat16 [64, 3584, 288], P(None, ('fsdp', 'sub'))
- owned_update: bfloat16 [64, 3584, 288], P(('fsdp', 'sub'))
Inputs may be any that keep to these rules, and one draw needn't show every extreme that they name: owner is a permutation: each group device owns exactly one matrix.
All inputs are finite; a program needn't handle non-finite values.
Results may differ from a plain program's by a relative error of at most 0.034.
Values may be sent and summed in bfloat16 or wider, within the bound.
No kernel may reach another device: no remote copies, remote signals or barrier semaphores. Data moves between devices by JAX's collectives and lax.ppermute only.
A program may use at most 64 MiB of HBM per device.

v0:
```python
import functools

import jax
import jax.numpy as jnp
from jax import lax
from jax.experimental import pallas as pl
from jax.experimental.pallas import tpu as pltpu
from jax.sharding import Mesh, PartitionSpec as P

ITERS = 3
GROUP = ("fsdp", "sub")
F32 = jnp.float32
BF16 = jnp.bfloat16
SLOTS_PER_STEP = 16
LANES = 128
SPARE = 16
NEAR = 3
VMEM_LIMIT = 32 * 1024 * 1024
SMEM = pl.BlockSpec(memory_space=pltpu.SMEM)
VMEM = pl.BlockSpec(memory_space=pltpu.VMEM)


def call(kernel, out_shape, n_in, scalars=0, scratch=(), flops=0, moved=4 << 20):
    several = isinstance(out_shape, (list, tuple))
    return pl.pallas_call(
        kernel,
        out_shape=out_shape,
        in_specs=[SMEM] * scalars + [VMEM] * n_in,
        out_specs=[VMEM] * len(out_shape) if several else VMEM,
        scratch_shapes=list(scratch),
        compiler_params=pltpu.CompilerParams(vmem_limit_bytes=VMEM_LIMIT),
        cost_estimate=pl.CostEstimate(flops=flops, bytes_accessed=moved, transcendentals=0),
    )


def shape(dims, dtype=BF16):
    return jax.ShapeDtypeStruct(dims, dtype)


def each(count, one, together=8):
    together = min(together, count)

    def several(k, carry):
        for i in range(together):
            one(k * together + i)
        return carry

    lax.fori_loop(0, count // together, several, 0)


def select_rows(first, count, width):
    row = lax.broadcasted_iota(jnp.int32, (count, width), 0)
    col = lax.broadcasted_iota(jnp.int32, (count, width), 1)
    return (col == row + first).astype(BF16)


def select_shares(share, width):
    row = lax.broadcasted_iota(jnp.int32, (width, width), 0)
    col = lax.broadcasted_iota(jnp.int32, (width, width), 1)
    reps = width // share
    picked = row
    for r in range(reps):
        hi, lo = r // NEAR, r % NEAR
        start = lo * (width // NEAR) + hi * share
        inside = (row >= r * share) & (row < (r + 1) * share)
        picked = jnp.where(inside, row + (start - r * share), picked)
    return (col == picked).astype(BF16)


def place_by_owner(owner_ref, x_ref, by_slot):
    def place(j):
        by_slot[owner_ref[j]] = x_ref[j].astype(F32)

    each(x_ref.shape[0], place)


def turned_part(pick, by_slot, k, step):
    _, rows, cols = by_slot.shape
    part = by_slot[k * step : (k + 1) * step].reshape(step * rows, cols).astype(BF16)
    return lax.dot_general(pick, part, (((1,), (1,)), ((), ())), preferred_element_type=F32)


def turn_grads_kernel(share, x_ref_owner, x_ref, out_ref, by_slot):
    count, rows, cols = x_ref.shape
    place_by_owner(x_ref_owner, x_ref, by_slot)
    pick = select_shares(share, cols)
    step = min(2 * SLOTS_PER_STEP, count)
    tiles = step * rows // LANES
    held = share * count * rows // LANES
    out_ref[...] = jnp.zeros(out_ref.shape, BF16)
    for k in range(count // step):
        turned = turned_part(pick, by_slot, k, step)
        for r in range(cols // share):
            mine = turned[r * share : (r + 1) * share]
            block = jnp.concatenate([mine[:, t * LANES : (t + 1) * LANES] for t in range(tiles)], axis=0)
            first = r * (held + SPARE) + k * tiles * share
            out_ref[first : first + tiles * share] = block.astype(BF16)


def turn_share_kernel(owner_ref, first_ref, x_ref, out_ref, by_slot):
    count, rows, cols = x_ref.shape
    place_by_owner(owner_ref, x_ref, by_slot)
    pick = select_rows(first_ref[0], out_ref.shape[0], cols)
    step = SLOTS_PER_STEP
    for k in range(count // step):
        out_ref[:, k * step * rows : (k + 1) * step * rows] = turned_part(pick, by_slot, k, step).astype(BF16)


def moment_kernel(count, total_ref, momentum_ref, new_ref, out_ref):
    rows_of = momentum_ref.shape[0]
    held = total_ref[...].astype(F32)
    total = jnp.concatenate([held[t : t + rows_of] for t in range(0, held.shape[0], rows_of)], axis=1)
    moment = 0.95 * momentum_ref[...].astype(F32) + total
    new_ref[...] = moment.astype(BF16)
    ahead = total + 0.95 * moment
    rows = total.shape[1] // count
    for s in range(count):
        block = ahead[:, s * rows : (s + 1) * rows].astype(BF16)
        out_ref[s, :, :rows] = block[:16]
        out_ref[s, :8, 64 : 64 + rows] = block[16:]


def join_kernel(x_ref, out_ref, whole):
    count = x_ref.shape[0]
    rows = out_ref.shape[1] // count
    for s in range(count):
        block = x_ref[s].astype(F32)
        whole[:16, s * rows : (s + 1) * rows] = block[:, :rows]
        whole[16:, s * rows : (s + 1) * rows] = block[:8, 64 : 64 + rows]
    out_ref[...] = whole[...].astype(BF16)


def untransposed(part, eye):
    return lax.dot_general(part, eye, (((0,), (0,)), ((), ())), preferred_element_type=F32)


def next_y(old, product):
    return (3.4445 * old.astype(F32) + product).astype(BF16)


def orthogonal_kernel(count, factor, third_ref, own_ref, before_ref, after_ref, packed_ref, y_ref, mixed_ref):
    third, length = own_ref.shape
    lo = third_ref[0]

    def of_third(which):
        return pl.ds(pl.multiple_of(lax.rem(which, NEAR) * third, third), third)

    y_ref[of_third(lo), :] = own_ref[...]
    y_ref[of_third(lo + NEAR - 1), :] = before_ref[...]
    y_ref[of_third(lo + 1), :] = after_ref[...]
    squares = jnp.zeros((1, 1), F32)
    for k in range(NEAR):
        value = y_ref[k * third : (k + 1) * third, :].astype(F32)
        squares += jnp.sum(value * value, keepdims=True)
    inverse = 1.0 / (jnp.sqrt(squares) + 1e-07)
    for k in range(NEAR):
        at = slice(k * third, (k + 1) * third)
        y_ref[at, :] = (y_ref[at, :].astype(F32) * inverse).astype(BF16)
    rows = length // count
    step = SLOTS_PER_STEP
    for it in range(ITERS):
        y = y_ref[...]
        gram = lax.dot_general(y, y, (((1,), (1,)), ((), ())), preferred_element_type=F32).astype(BF16)
        square = jnp.dot(gram, gram, preferred_element_type=F32)
        mixed = (-4.775 * gram.astype(F32) + 2.0315 * square).astype(BF16)
        if it == ITERS - 1:
            break
        for k in range(count // step):
            at = slice(k * step * rows, (k + 1) * step * rows)
            y_ref[:, at] = next_y(y_ref[:, at], jnp.dot(mixed, y_ref[:, at], preferred_element_type=F32))
    mixed_ref[...] = mixed
    mine = mixed_ref[of_third(lo), :]
    eye = select_rows(0, third, third)
    top = rows - 8
    for k in range(count // step):
        at = slice(k * step * rows, (k + 1) * step * rows)
        new = next_y(y_ref[of_third(lo), at], jnp.dot(mine, y_ref[:, at], preferred_element_type=F32))
        update = untransposed((factor * new.astype(F32)).astype(BF16), eye).reshape(step, rows, third)
        low = [update[:, top:, 32 * j : 32 * j + 32] for j in range(third // 32)]
        low.append(jnp.zeros((step, top - 8 * len(low), 32), F32))
        block = jnp.concatenate([update[:, :top], jnp.concatenate(low, axis=1)], axis=2)
        packed_ref[k * step : (k + 1) * step] = block.astype(BF16)


def owned_kernel(count, factor, y_ref, mixed_ref, owned_ref):
    width = SLOTS_PER_STEP * y_ref.shape[1] // count
    for k in range(y_ref.shape[1] // width):
        at = slice(k * width, (k + 1) * width)
        new = next_y(y_ref[:, at], jnp.dot(mixed_ref[...], y_ref[:, at], preferred_element_type=F32))
        owned_ref[:, at] = (factor * new.astype(F32)).astype(BF16)


def unpack_kernel(owner_ref, third_ref, own_ref, before_ref, after_ref, out_ref):
    count, rows, cols = out_ref.shape
    start = pl.program_id(0) * count
    third = cols // NEAR
    top = rows - 8

    def columns(block):
        low = [block[8 * k : 8 * k + 8, third:] for k in range(third // 32)]
        return jnp.concatenate([block[:top, :third], jnp.concatenate(low, axis=1)], axis=0)

    for lo in range(NEAR):

        @pl.when(third_ref[0] == lo)
        def _():
            refs = [None] * NEAR
            refs[lo], refs[(lo + NEAR - 1) % NEAR], refs[(lo + 1) % NEAR] = own_ref, before_ref, after_ref

            def one(j):
                slot = owner_ref[start + j]
                parts = [columns(ref[slot].astype(F32)) for ref in refs]
                out_ref[j] = jnp.concatenate(parts, axis=1).astype(BF16)

            each(count, one, 4)


def unpack(owner, lo, own, before, after, out):
    count, rows, cols = out.shape
    together = min(SLOTS_PER_STEP, count)
    whole = pl.BlockSpec(own.shape, lambda k: (0, 0, 0))
    return pl.pallas_call(
        unpack_kernel,
        out_shape=out,
        grid=(count // together,),
        in_specs=[SMEM, SMEM, whole, whole, whole],
        out_specs=pl.BlockSpec((together, rows, cols), lambda k: (k, 0, 0)),
        compiler_params=pltpu.CompilerParams(vmem_limit_bytes=VMEM_LIMIT),
        cost_estimate=pl.CostEstimate(flops=0, bytes_accessed=4 << 20, transcendentals=0),
    )(owner, lo, own, before, after)


def unturn_kernel(share, owner_ref, x_ref, out_ref, by_slot):
    count, rows, cols = out_ref.shape
    step = SLOTS_PER_STEP
    pick = select_shares(share, cols)
    for k in range(count // step):
        part = untransposed(x_ref[:, k * step * rows : (k + 1) * step * rows], pick)
        by_slot[k * step : (k + 1) * step] = part.reshape(step, rows, cols)

    def one(j):
        out_ref[j] = by_slot[owner_ref[j]].astype(BF16)

    each(count, one)


def with_neighbours(part):
    reps = lax.axis_size("hi") * lax.axis_size("lo")
    before = lax.ppermute(part, ("hi", "lo"), [(r, (r + 1) % reps) for r in range(reps)])
    after = lax.ppermute(part, ("hi", "lo"), [((r + 1) % reps, r) for r in range(reps)])
    return part, before, after


def body(grads, momentum, owner):
    _, count, rows, cols = grads.shape
    reps = lax.axis_size("hi") * lax.axis_size("lo")
    share = cols // reps
    third = cols // NEAR
    length = count * rows
    hi, lo = lax.axis_index("hi").astype(jnp.int32), lax.axis_index("lo").astype(jnp.int32)
    first = (lo * third + hi * share).reshape(1)
    lo = lo.reshape(1)
    by_slot = [pltpu.VMEM((count, rows, cols), F32)]
    held = share * length // LANES
    turned = call(
        functools.partial(turn_grads_kernel, share),
        shape((reps * (held + SPARE - 1), LANES)),
        1,
        scalars=1,
        scratch=by_slot,
        flops=2 * length * cols * cols,
    )(owner, grads[0])
    total = lax.psum_scatter(turned, ("hi", "lo"), scatter_dimension=0, tiled=True)
    total = lax.optimization_barrier(total)
    total = lax.dynamic_slice(total, (lax.axis_index(("hi", "lo")), 0), (held, LANES))
    mine = call(
        turn_share_kernel, shape((share, length)), 1, scalars=2, scratch=by_slot, flops=2 * length * cols * share
    )(owner, first, momentum)
    new_share, outgoing = call(
        functools.partial(moment_kernel, count), [shape((share, length)), shape((count, 16, 128))], 2
    )(total, mine)
    arrived = lax.all_to_all(outgoing, GROUP, split_axis=0, concat_axis=0, tiled=True)
    joined = call(join_kernel, shape((share, length)), 1, scratch=[pltpu.VMEM((share, length), F32)])(arrived)
    own = lax.all_gather(joined, "hi", axis=0, tiled=True)
    own, before, after = with_neighbours(own)
    own, before, after, new_share = lax.optimization_barrier((own, before, after, new_share))
    new_turned = lax.all_gather(new_share, ("hi", "lo"), axis=0, tiled=True)
    factor = 0.2 * max(length, cols) ** 0.5
    packed, last, mixed = call(
        functools.partial(orthogonal_kernel, count, factor),
        [shape((count, rows - 8, third + 32)), shape((cols, length)), shape((cols, cols))],
        3,
        scalars=1,
        flops=4 * ITERS * length * cols * cols,
    )(lo, own, before, after)
    returned = lax.all_to_all(packed, GROUP, split_axis=0, concat_axis=0, tiled=True)
    returned = with_neighbours(returned)
    owned = call(
        functools.partial(owned_kernel, count, factor), shape((cols, length)), 2, flops=2 * length * cols * cols
    )(last, mixed)
    new_turned, owned = lax.optimization_barrier((new_turned, owned))
    new_momentum = call(
        functools.partial(unturn_kernel, share),
        shape((count, rows, cols)),
        1,
        scalars=1,
        scratch=by_slot,
        flops=2 * length * cols * cols,
    )(owner, new_turned)
    *returned, new_momentum = lax.optimization_barrier((*returned, new_momentum))
    update = unpack(owner, lo, *returned, shape((count, rows, cols)))
    return (new_momentum, update, owned.T[None])


def solution(mesh):
    reps, fsdp, sub = mesh.devices.shape
    mesh = Mesh(mesh.devices.reshape(reps // NEAR, NEAR, fsdp, sub), ("hi", "lo") + GROUP)
    return jax.shard_map(
        body,
        mesh=mesh,
        in_specs=(P(("hi", "lo"), None, GROUP, None), P(None, GROUP, None), P()),
        out_specs=(P(None, GROUP, None), P(None, GROUP, None), P(GROUP, None, None)),
        check_vma=False,
    )
```

profile of v0, /device:TPU:1, one launch (start us, length us, event | category | flops | bytes accessed | tf_op | source)
XLA Modules:
  0.0 211.0 jit_solution(15359060510034570031)
XLA Ops:
  7.2 1.8 copy-done
  9.6 2.5 %shard_map.58 = bf16[8244,128]{1,0:T(8,128)(2,1)S(1)} custom-call(s32[64]{0:T(128)S(1)} %copy-done.3, bf16[64,56,288]{2,1,0:T(8,128)(2,1)S(1)} %bitcast.9), custom_call_target="tpu_custom_call" | custom-call | flops 594542592 | bytes 4194304 | tf_op jit(solution)/shard_map/pallas_call | solution.py:265
  12.1 40.1 %fusion = bf16[688,128]{1,0:T(8,128)(2,1)S(1)} fusion(bf16[8244,128]{1,0:T(8,128)(2,1)S(1)} %shard_map.58), kind=kCustom, calls=%all-reduce-scatter | all-reduce-scatter fusion | flops 1056769 | bytes 2290688
  52.2 1.8 collective-permute-start.4
  54.0 1.3 dynamic-slice.4
  56.0 1.8 copy-done.1
  57.7 1.9 shard_map.59.momentum_ref
  61.6 26.5 %all_to_all.10.x_ref = bf16[64,16,128]{2,1,0:T(8,128)(2,1)S(1)} all-to-all(bf16[64,16,128]{2,1,0:T(8,128)(2,1)S(1)} %get-tuple-element.18), channel_id=1, replica_groups=mesh['hi'=4,'lo'=3,'fsdp'=32,'sub'=2] {'fsdp','sub'}, dimensions={0} | all-to-all | bytes 524288 | tf_op jit(solution)/shard_map/all_to_all | solution.py:282
  88.3 23.6 %all_gather.6.own_ref = bf16[96,3584]{1,0:T(8,128)(2,1)S(1)} all-gather(bf16[24,3584]{1,0:T(8,128)(2,1)S(1)} %shard_map.61), channel_id=1, replica_groups=mesh['hi'=4,'lo'=3,'fsdp'=32,'sub'=2] {'hi'}, dimensions={0}, use_global_device_ids=true | all-gather | bytes 860160 | tf_op jit(solution)/shard_map/all_gather | solution.py:284
  111.9 1.9 collective-permute-start.1
  113.8 4.0 %collective-permute-start = (bf16[96,3584]{1,0:T(8,128)(2,1)S(1)}, bf16[96,3584]{1,0:T(8,128)(2,1)S(1)}, u32[]{:S(2)}, u32[]{:S(2)}) collective-permute-start(bf16[96,3584]{1,0:T(8,128)(2,1)S(1)} %all_gather.6.own_ref), channel_id=1, source_target_pairs={{0,64},{64,128},{128,192},{192,256},{256,320},{320,384},{384,448},... | collective-permute-start | bytes 2064392 | tf_op jit(solution)/shard_map/ppermute | solution.py:249
  117.8 11.7 %collective-permute-done.1.after_ref = bf16[96,3584]{1,0:T(8,128)(2,1)S(1)} collective-permute-done((bf16[96,3584]{1,0:T(8,128)(2,1)S(1)}, bf16[96,3584]{1,0:T(8,128)(2,1)S(1)}, u32[]{:S(2)}, u32[]{:S(2)}) %collective-permute-start.1) | collective-permute-done | bytes 688160 | tf_op jit(solution)/shard_map/ppermute | solution.py:250
  129.6 1.5 collective-permute-done.before_ref
  131.1 9.4 %shard_map.62 = (bf16[64,48,128]{2,1,0:T(8,128)(2,1)S(1)}, bf16[288,3584]{1,0:T(8,128)(2,1)S(1)}, bf16[288,288]{1,0:T(8,128)(2,1)S(1)}) custom-call(s32[1]{0:T(128)} %bitcast.third_ref, bf16[96,3584]{1,0:T(8,128)(2,1)S(1)} %all_gather.6.own_ref, bf16[96,3584]{1,0:T(8,128)(2,1)S(1)} %collective-permute-done.before_ref, ...), custom_call_target="tpu_custom_call" | custom-call | flops 3567255552 | bytes 4194304 | tf_op jit(solution)/shard_map/pallas_call | solution.py:289
  140.5 32.4 %all_to_all.11.own_ref = bf16[64,48,128]{2,1,0:T(8,128)(2,1)S(1)} all-to-all(bf16[64,48,128]{2,1,0:T(8,128)(2,1)S(1)} %get-tuple-element.23), channel_id=1, replica_groups=mesh['hi'=4,'lo'=3,'fsdp'=32,'sub'=2] {'fsdp','sub'}, dimensions={0} | all-to-all | bytes 1572864 | tf_op jit(solution)/shard_map/all_to_all | solution.py:296
  172.9 3.2 %collective-permute-start.3 = (bf16[64,48,128]{2,1,0:T(8,128)(2,1)S(1)}, bf16[64,48,128]{2,1,0:T(8,128)(2,1)S(1)}, u32[]{:S(2)}, u32[]{:S(2)}) collective-permute-start(bf16[64,48,128]{2,1,0:T(8,128)(2,1)S(1)} %all_to_all.11.own_ref), channel_id=1, source_target_pairs={{64,0},{128,64},{192,128},{256,192},{320,256},{384,320},{448,384},... | collective-permute-start | bytes 2359304 | tf_op jit(solution)/shard_map/ppermute | solution.py:250
  176.2 2.1 collective-permute-start.2
  178.2 2.7 %shard_map.63 = bf16[288,3584]{1,0:T(8,128)(2,1)} custom-call(bf16[288,3584]{1,0:T(8,128)(2,1)S(1)} %get-tuple-element.25.y_ref, bf16[288,288]{1,0:T(8,128)(2,1)S(1)} %get-tuple-element.26.mixed_ref), custom_call_target="tpu_custom_call" | custom-call | flops 594542592 | bytes 4194304 | tf_op jit(solution)/shard_map/pallas_call | solution.py:298
  180.9 1.5 all-gather.2.cloned.1.call-done.x_ref
  182.5 1.6 copy-done.2
  184.0 4.3 %shard_map.64 = bf16[64,56,288]{2,1,0:T(8,128)(2,1)} custom-call(s32[64]{0:T(128)S(1)} %copy-done.4, bf16[288,3584]{1,0:T(8,128)(2,1)S(1)} %copy-done.2), custom_call_target="tpu_custom_call" | custom-call | flops 594542592 | bytes 4194304 | tf_op jit(solution)/shard_map/pallas_call | solution.py:302
  188.3 9.4 %collective-permute-done.3.after_ref = bf16[64,48,128]{2,1,0:T(8,128)(2,1)S(1)} collective-permute-done((bf16[64,48,128]{2,1,0:T(8,128)(2,1)S(1)}, bf16[64,48,128]{2,1,0:T(8,128)(2,1)S(1)}, u32[]{:S(2)}, u32[]{:S(2)}) %collective-permute-start.3) | collective-permute-done | bytes 786464 | tf_op jit(solution)/shard_map/ppermute | solution.py:250
  197.8 1.3 collective-permute-done.2.before_ref
  199.0 5.1 %shard_map.65 = bf16[64,56,288]{2,1,0:T(8,128)(2,1)} custom-call(s32[64]{0:T(128)S(1)} %copy-done.4, s32[1]{0:T(128)} %bitcast.third_ref, bf16[64,48,128]{2,1,0:T(8,128)(2,1)S(1)} %all_to_all.11.own_ref, bf16[64,48,128]{2,1,0:T(8,128)(2,1)S(1)} %collective-permute-done.2.before_ref, bf16[64,48,128]{2,1,0:T(8,128)(2,1)S(1)} %collective-permute-done.3.after_ref), custom_call_target="tpu_custom_call" | custom-call | bytes 4194304 | tf_op jit(solution)/shard_map/pallas_call | solution.py:222
  (16 shorter events, 2.9 us)
Async XLA Ops:
  7.2 175.3 %all-gather.2.cloned.1.call-start = ((), (), s32[]{:S(2)}) async-start(), calls=%async_computation.2 | async-start | bytes 2236416 | tf_op jit(solution)/shard_map/all_gather | solution.py:287
  7.2 1.8 copy-start
  9.0 0.7 copy-start.3
  12.1 43.8 %copy-start.4 = (s32[64]{0:T(128)S(1)}, s32[64]{0:T(128)}, u32[]{:S(2)}) copy-start(s32[64]{0:T(128)} %owner_ref.5) | copy-start | bytes 772
  52.2 7.4 %collective-permute-start.4 = (bf16[11,128]{1,0:T(8,128)(2,1)S(1)}, bf16[11,128]{1,0:T(8,128)(2,1)S(1)}, u32[]{:S(2)}, u32[]{:S(2)}) collective-permute-start(bf16[11,128]{1,0:T(8,128)(2,1)S(1)} %slice), channel_id=1, source_target_pairs={{0,64},{64,128},{128,192},{192,256},{256,320},{320,384},{384,448},... | collective-permute-start | bytes 8456
  55.9 1.8 copy-start.1
  111.9 17.7 %collective-permute-start.1 = (bf16[96,3584]{1,0:T(8,128)(2,1)S(1)}, bf16[96,3584]{1,0:T(8,128)(2,1)S(1)}, u32[]{:S(2)}, u32[]{:S(2)}) collective-permute-start(bf16[96,3584]{1,0:T(8,128)(2,1)S(1)} %all_gather.6.own_ref), channel_id=1, source_target_pairs={{64,0},{128,64},{192,128},{256,192},{320,256},{384,320},{448,384},... | collective-permute-start | bytes 2064392 | tf_op jit(solution)/shard_map/ppermute | solution.py:250
  113.8 17.2 %collective-permute-start = (bf16[96,3584]{1,0:T(8,128)(2,1)S(1)}, bf16[96,3584]{1,0:T(8,128)(2,1)S(1)}, u32[]{:S(2)}, u32[]{:S(2)}) collective-permute-start(bf16[96,3584]{1,0:T(8,128)(2,1)S(1)} %all_gather.6.own_ref), channel_id=1, source_target_pairs={{0,64},{64,128},{128,192},{192,256},{256,320},{320,384},{384,448},... | collective-permute-start | bytes 2064392 | tf_op jit(solution)/shard_map/ppermute | solution.py:249
  172.9 24.8 %collective-permute-start.3 = (bf16[64,48,128]{2,1,0:T(8,128)(2,1)S(1)}, bf16[64,48,128]{2,1,0:T(8,128)(2,1)S(1)}, u32[]{:S(2)}, u32[]{:S(2)}) collective-permute-start(bf16[64,48,128]{2,1,0:T(8,128)(2,1)S(1)} %all_to_all.11.own_ref), channel_id=1, source_target_pairs={{64,0},{128,64},{192,128},{256,192},{320,256},{384,320},{448,384},... | collective-permute-start | bytes 2359304 | tf_op jit(solution)/shard_map/ppermute | solution.py:250
  176.2 22.9 %collective-permute-start.2 = (bf16[64,48,128]{2,1,0:T(8,128)(2,1)S(1)}, bf16[64,48,128]{2,1,0:T(8,128)(2,1)S(1)}, u32[]{:S(2)}, u32[]{:S(2)}) collective-permute-start(bf16[64,48,128]{2,1,0:T(8,128)(2,1)S(1)} %all_to_all.11.own_ref), channel_id=1, source_target_pairs={{0,64},{64,128},{128,192},{192,256},{256,320},{320,384},{384,448},... | collective-permute-start | bytes 2359304 | tf_op jit(solution)/shard_map/ppermute | solution.py:249
  182.5 1.6 copy-start.2
Sparse Core Ops, SparseCore 0:
  131.2 51.2 all-gather.1
where the time goes:
time: 212 us; the launch traced here: 211 us
  blocking collectives  123 us (58%)
  Pallas kernels  26.9 us (13%)
  waiting for transfers between devices  25.5 us (12%)
  between operations  14.8 us (7%)
  starting transfers between devices  13 us (6%)
  local copies, waits for them, and re-layouts  8.11 us (4%)
    unnamed x1, blocking collectives  40.1 us
    all_to_all x1, blocking collectives, body(): lax.all_to_all(packed, GROUP, split_axis=0, concat_axis=0, tiled=True)  32.4 us
    all_to_all x1, blocking collectives, body(): lax.all_to_all(outgoing, GROUP, split_axis=0, concat_axis=0, tiled=True)  26.5 us
    all_gather x1, blocking collectives, body(): own = lax.all_gather(joined, 'hi', axis=0, tiled=True)  23.6 us
    ppermute x2, waiting for transfers between devices, with_neighbours(): lax.ppermute(part, ('hi', 'lo'), [((r + 1) % reps, r) for r in range(reps)])  21.2 us
    pallas_call x1, Pallas kernels, body(): call(functools.partial(orthogonal_kernel, count, factor), [shape((count,...  9.41 us
    unnamed x14, local copies, waits for them, and re-layouts  8.06 us
    ppermute x2, starting transfers between devices, with_neighbours(): lax.ppermute(part, ('hi', 'lo'), [(r, (r + 1) % reps) for r in range(reps)])  6.05 us
  transfers between devices with their start and end apart: 6, of which 5 were waited for; matrix products, arithmetic and copies ran while one was open for 1% of the time, Pallas kernels for 9%

commit v1 on v0

--- a/solution.py
+++ b/solution.py
@@ -15,7 +15,7 @@
 LANES = 128
 SPARE = 16
 NEAR = 3
-VMEM_LIMIT = 32 * 1024 * 1024
+VMEM_LIMIT = 20 * 1024 * 1024
 SMEM = pl.BlockSpec(memory_space=pltpu.SMEM)
 VMEM = pl.BlockSpec(memory_space=pltpu.VMEM)
 
@@ -87,7 +87,9 @@
     step = min(2 * SLOTS_PER_STEP, count)
     tiles = step * rows // LANES
     held = share * count * rows // LANES
-    out_ref[...] = jnp.zeros(out_ref.shape, BF16)
+    for r in range(cols // share):
+        after = slice(r * (held + SPARE) + held, min((r + 1) * (held + SPARE), out_ref.shape[0]))
+        out_ref[after] = jnp.zeros((after.stop - after.start, LANES), BF16)
     for k in range(count // step):
         turned = turned_part(pick, by_slot, k, step)
         for r in range(cols // share):

time: 212 us -> 211 us (level)
  no operation moved by 1% of the time
where the time goes in v1:
time: 211 us
  blocking collectives  122 us (58%)
  Pallas kernels  26.6 us (13%)
  waiting for transfers between devices  25.5 us (12%)
  between operations  14.8 us (7%)
  starting transfers between devices  13 us (6%)
  local copies, waits for them, and re-layouts  8.11 us (4%)
    unnamed x1, blocking collectives  40.1 us
    all_to_all x1, blocking collectives, body(): lax.all_to_all(packed, GROUP, split_axis=0, concat_axis=0, tiled=True)  32.3 us
    all_to_all x1, blocking collectives, body(): lax.all_to_all(outgoing, GROUP, split_axis=0, concat_axis=0, tiled=True)  26.5 us
    all_gather x1, blocking collectives, body(): own = lax.all_gather(joined, 'hi', axis=0, tiled=True)  23.6 us
    ppermute x2, waiting for transfers between devices, with_neighbours(): lax.ppermute(part, ('hi', 'lo'), [((r + 1) % reps, r) for r in range(reps)])  20.9 us
    pallas_call x1, Pallas kernels, body(): call(functools.partial(orthogonal_kernel, count, factor), [shape((count,...  9.41 us
    unnamed x14, local copies, waits for them, and re-layouts  8.06 us
    ppermute x2, starting transfers between devices, with_neighbours(): lax.ppermute(part, ('hi', 'lo'), [(r, (r + 1) % reps) for r in range(reps)])  6.08 us
  transfers between devices with their start and end apart: 6, of which 5 were waited for; matrix products, arithmetic and copies ran while one was open for 1% of the time, Pallas kernels for 9%

profile of v1, /device:TPU:1, one launch (start us, length us, event | category | flops | bytes accessed | tf_op | source)
XLA Modules:
  0.0 210.5 jit_solution(5818913008807208457)
XLA Ops:
  7.2 1.8 copy-done
  9.6 2.2 %shard_map.58 = bf16[8244,128]{1,0:T(8,128)(2,1)S(1)} custom-call(s32[64]{0:T(128)S(1)} %copy-done.3, bf16[64,56,288]{2,1,0:T(8,128)(2,1)S(1)} %bitcast.9), custom_call_target="tpu_custom_call" | custom-call | flops 594542592 | bytes 4194304 | tf_op jit(solution)/shard_map/pallas_call | solution.py:267
  11.9 40.1 %fusion = bf16[688,128]{1,0:T(8,128)(2,1)S(1)} fusion(bf16[8244,128]{1,0:T(8,128)(2,1)S(1)} %shard_map.58), kind=kCustom, calls=%all-reduce-scatter | all-reduce-scatter fusion | flops 1056769 | bytes 2290688
  52.0 1.8 collective-permute-start.4
  53.7 1.3 dynamic-slice.4
  55.7 1.8 copy-done.1
  57.5 1.9 shard_map.59.momentum_ref
  61.3 26.5 %all_to_all.10.x_ref = bf16[64,16,128]{2,1,0:T(8,128)(2,1)S(1)} all-to-all(bf16[64,16,128]{2,1,0:T(8,128)(2,1)S(1)} %get-tuple-element.18), channel_id=1, replica_groups=mesh['hi'=4,'lo'=3,'fsdp'=32,'sub'=2] {'fsdp','sub'}, dimensions={0} | all-to-all | bytes 524288 | tf_op jit(solution)/shard_map/all_to_all | solution.py:284
  88.0 23.6 %all_gather.6.own_ref = bf16[96,3584]{1,0:T(8,128)(2,1)S(1)} all-gather(bf16[24,3584]{1,0:T(8,128)(2,1)S(1)} %shard_map.61), channel_id=1, replica_groups=mesh['hi'=4,'lo'=3,'fsdp'=32,'sub'=2] {'hi'}, dimensions={0}, use_global_device_ids=true | all-gather | bytes 860160 | tf_op jit(solution)/shard_map/all_gather | solution.py:286
  111.6 1.9 collective-permute-start.1
  113.6 4.0 %collective-permute-start = (bf16[96,3584]{1,0:T(8,128)(2,1)S(1)}, bf16[96,3584]{1,0:T(8,128)(2,1)S(1)}, u32[]{:S(2)}, u32[]{:S(2)}) collective-permute-start(bf16[96,3584]{1,0:T(8,128)(2,1)S(1)} %all_gather.6.own_ref), channel_id=1, source_target_pairs={{0,64},{64,128},{128,192},{192,256},{256,320},{320,384},{384,448},... | collective-permute-start | bytes 2064392 | tf_op jit(solution)/shard_map/ppermute | solution.py:251
  117.6 11.7 %collective-permute-done.1.after_ref = bf16[96,3584]{1,0:T(8,128)(2,1)S(1)} collective-permute-done((bf16[96,3584]{1,0:T(8,128)(2,1)S(1)}, bf16[96,3584]{1,0:T(8,128)(2,1)S(1)}, u32[]{:S(2)}, u32[]{:S(2)}) %collective-permute-start.1) | collective-permute-done | bytes 688160 | tf_op jit(solution)/shard_map/ppermute | solution.py:252
  129.3 1.5 collective-permute-done.before_ref
  130.8 9.4 %shard_map.62 = (bf16[64,48,128]{2,1,0:T(8,128)(2,1)S(1)}, bf16[288,3584]{1,0:T(8,128)(2,1)S(1)}, bf16[288,288]{1,0:T(8,128)(2,1)S(1)}) custom-call(s32[1]{0:T(128)} %bitcast.third_ref, bf16[96,3584]{1,0:T(8,128)(2,1)S(1)} %all_gather.6.own_ref, bf16[96,3584]{1,0:T(8,128)(2,1)S(1)} %collective-permute-done.before_ref, ...), custom_call_target="tpu_custom_call" | custom-call | flops 3567255552 | bytes 4194304 | tf_op jit(solution)/shard_map/pallas_call | solution.py:291
  140.2 32.3 %all_to_all.11.own_ref = bf16[64,48,128]{2,1,0:T(8,128)(2,1)S(1)} all-to-all(bf16[64,48,128]{2,1,0:T(8,128)(2,1)S(1)} %get-tuple-element.23), channel_id=1, replica_groups=mesh['hi'=4,'lo'=3,'fsdp'=32,'sub'=2] {'fsdp','sub'}, dimensions={0} | all-to-all | bytes 1572864 | tf_op jit(solution)/shard_map/all_to_all | solution.py:298
  172.5 3.2 %collective-permute-start.3 = (bf16[64,48,128]{2,1,0:T(8,128)(2,1)S(1)}, bf16[64,48,128]{2,1,0:T(8,128)(2,1)S(1)}, u32[]{:S(2)}, u32[]{:S(2)}) collective-permute-start(bf16[64,48,128]{2,1,0:T(8,128)(2,1)S(1)} %all_to_all.11.own_ref), channel_id=1, source_target_pairs={{64,0},{128,64},{192,128},{256,192},{320,256},{384,320},{448,384},... | collective-permute-start | bytes 2359304 | tf_op jit(solution)/shard_map/ppermute | solution.py:252
  175.7 2.1 collective-permute-start.2
  177.8 2.7 %shard_map.63 = bf16[288,3584]{1,0:T(8,128)(2,1)} custom-call(bf16[288,3584]{1,0:T(8,128)(2,1)S(1)} %get-tuple-element.25.y_ref, bf16[288,288]{1,0:T(8,128)(2,1)S(1)} %get-tuple-element.26.mixed_ref), custom_call_target="tpu_custom_call" | custom-call | flops 594542592 | bytes 4194304 | tf_op jit(solution)/shard_map/pallas_call | solution.py:300
  180.5 1.6 all-gather.2.cloned.1.call-done.x_ref
  182.1 1.6 copy-done.2
  183.7 4.3 %shard_map.64 = bf16[64,56,288]{2,1,0:T(8,128)(2,1)} custom-call(s32[64]{0:T(128)S(1)} %copy-done.4, bf16[288,3584]{1,0:T(8,128)(2,1)S(1)} %copy-done.2), custom_call_target="tpu_custom_call" | custom-call | flops 594542592 | bytes 4194304 | tf_op jit(solution)/shard_map/pallas_call | solution.py:304
  188.0 9.2 %collective-permute-done.3.after_ref = bf16[64,48,128]{2,1,0:T(8,128)(2,1)S(1)} collective-permute-done((bf16[64,48,128]{2,1,0:T(8,128)(2,1)S(1)}, bf16[64,48,128]{2,1,0:T(8,128)(2,1)S(1)}, u32[]{:S(2)}, u32[]{:S(2)}) %collective-permute-start.3) | collective-permute-done | bytes 786464 | tf_op jit(solution)/shard_map/ppermute | solution.py:252
  197.2 1.4 collective-permute-done.2.before_ref
  198.6 5.1 %shard_map.65 = bf16[64,56,288]{2,1,0:T(8,128)(2,1)} custom-call(s32[64]{0:T(128)S(1)} %copy-done.4, s32[1]{0:T(128)} %bitcast.third_ref, bf16[64,48,128]{2,1,0:T(8,128)(2,1)S(1)} %all_to_all.11.own_ref, bf16[64,48,128]{2,1,0:T(8,128)(2,1)S(1)} %collective-permute-done.2.before_ref, bf16[64,48,128]{2,1,0:T(8,128)(2,1)S(1)} %collective-permute-done.3.after_ref), custom_call_target="tpu_custom_call" | custom-call | bytes 4194304 | tf_op jit(solution)/shard_map/pallas_call | solution.py:224
  (16 shorter events, 2.9 us)
Async XLA Ops:
  7.2 175.0 %all-gather.2.cloned.1.call-start = ((), (), s32[]{:S(2)}) async-start(), calls=%async_computation.2 | async-start | bytes 2236416 | tf_op jit(solution)/shard_map/all_gather | solution.py:289
  7.2 1.8 copy-start
  9.0 0.7 copy-start.3
  11.9 43.8 %copy-start.4 = (s32[64]{0:T(128)S(1)}, s32[64]{0:T(128)}, u32[]{:S(2)}) copy-start(s32[64]{0:T(128)} %owner_ref.5) | copy-start | bytes 772
  52.0 7.4 %collective-permute-start.4 = (bf16[11,128]{1,0:T(8,128)(2,1)S(1)}, bf16[11,128]{1,0:T(8,128)(2,1)S(1)}, u32[]{:S(2)}, u32[]{:S(2)}) collective-permute-start(bf16[11,128]{1,0:T(8,128)(2,1)S(1)} %slice), channel_id=1, source_target_pairs={{0,64},{64,128},{128,192},{192,256},{256,320},{320,384},{384,448},... | collective-permute-start | bytes 8456
  55.7 1.8 copy-start.1
  111.6 17.7 %collective-permute-start.1 = (bf16[96,3584]{1,0:T(8,128)(2,1)S(1)}, bf16[96,3584]{1,0:T(8,128)(2,1)S(1)}, u32[]{:S(2)}, u32[]{:S(2)}) collective-permute-start(bf16[96,3584]{1,0:T(8,128)(2,1)S(1)} %all_gather.6.own_ref), channel_id=1, source_target_pairs={{64,0},{128,64},{192,128},{256,192},{320,256},{384,320},{448,384},... | collective-permute-start | bytes 2064392 | tf_op jit(solution)/shard_map/ppermute | solution.py:252
  113.6 17.2 %collective-permute-start = (bf16[96,3584]{1,0:T(8,128)(2,1)S(1)}, bf16[96,3584]{1,0:T(8,128)(2,1)S(1)}, u32[]{:S(2)}, u32[]{:S(2)}) collective-permute-start(bf16[96,3584]{1,0:T(8,128)(2,1)S(1)} %all_gather.6.own_ref), channel_id=1, source_target_pairs={{0,64},{64,128},{128,192},{192,256},{256,320},{320,384},{384,448},... | collective-permute-start | bytes 2064392 | tf_op jit(solution)/shard_map/ppermute | solution.py:251
  172.5 24.7 %collective-permute-start.3 = (bf16[64,48,128]{2,1,0:T(8,128)(2,1)S(1)}, bf16[64,48,128]{2,1,0:T(8,128)(2,1)S(1)}, u32[]{:S(2)}, u32[]{:S(2)}) collective-permute-start(bf16[64,48,128]{2,1,0:T(8,128)(2,1)S(1)} %all_to_all.11.own_ref), channel_id=1, source_target_pairs={{64,0},{128,64},{192,128},{256,192},{320,256},{384,320},{448,384},... | collective-permute-start | bytes 2359304 | tf_op jit(solution)/shard_map/ppermute | solution.py:252
  175.7 22.9 %collective-permute-start.2 = (bf16[64,48,128]{2,1,0:T(8,128)(2,1)S(1)}, bf16[64,48,128]{2,1,0:T(8,128)(2,1)S(1)}, u32[]{:S(2)}, u32[]{:S(2)}) collective-permute-start(bf16[64,48,128]{2,1,0:T(8,128)(2,1)S(1)} %all_to_all.11.own_ref), channel_id=1, source_target_pairs={{0,64},{64,128},{128,192},{192,256},{256,320},{320,384},{384,448},... | collective-permute-start | bytes 2359304 | tf_op jit(solution)/shard_map/ppermute | solution.py:251
  182.1 1.6 copy-start.2
Sparse Core Ops, SparseCore 0:
  130.9 51.1 all-gather.1
